TPU v7x, 32 devices: a whole 2x2x4 slice. The times are simulated.
32 devices in a mesh: row: 8 (over z, y), col: 4 (over x, core).
Axes of the slice: x: 2, y: 2, z: 4, core: 2. Of those that a mesh axis runs over, the one named last changes fastest.
Arguments:
- fit_tiles: bfloat16 [16, 24, 128, 128], P('row', 'col'), may hold values from -6 to 6
- aux_list: int32 [16, 24], P('row', 'col'), may hold values from 0 to 11, as said below
- aux_count: int32 [16, 4], P('row', 'col'), may hold values from 1 to 6, as said below
- metric: bfloat16 [48, 128, 128], P('col', 'row'), may hold values from -0.5 to 0.5
Outputs:
- exchange: float32 [2048, 2048], P('col', 'row')
Inputs may be any that keep to these rules, and one draw needn't show every extreme that they name: `aux_list`: within one atom block and one col shard, the first 6 slots name distinct auxiliary blocks. `aux_count`: counts follow a density per atom block; the largest is reached in every draw.
All inputs are finite; a program needn't handle non-finite values.
Results may differ from a plain program's by a relative error of at most 0.0015.
Values may be sent and summed in bfloat16 or wider, within the bound.
A program may use at most 64 MiB of HBM per device.

v0:
```python
import jax
import jax.numpy as jnp
from jax import lax
from jax.sharding import PartitionSpec as P

AUXB = 128
QS = 6


def expand(fitted, marked, local_aux):
    onehot = (marked[:, :, None] == jnp.arange(local_aux, dtype=jnp.int32)[None, None, :]).astype(
        jnp.bfloat16
    )
    dense = jnp.einsum("asq,asmn->amqn", onehot, fitted, preferred_element_type=jnp.float32).astype(
        jnp.bfloat16
    )
    return dense.reshape(fitted.shape[0] * fitted.shape[2], local_aux * fitted.shape[3])


def local(fit_tiles, aux_list, aux_count, metric):
    slots = fit_tiles.shape[1]
    local_aux = metric.shape[0]
    full_metric = lax.all_gather(metric, "row", axis=1, tiled=True)
    alive = jnp.arange(slots, dtype=jnp.int32)[None, :] < aux_count
    marked = jnp.where(alive, aux_list, local_aux)
    picked = full_metric[aux_list]
    fitted = jnp.einsum(
        "asmk,askn->asmn", fit_tiles, picked, preferred_element_type=jnp.float32
    ).astype(jnp.bfloat16)
    dense = expand(fitted, marked, local_aux)
    factor = 1.0 / (QS * lax.axis_size("col") * AUXB) ** 0.5
    gathered = lax.all_gather(dense, "row", axis=0, tiled=True)
    summed = lax.psum_scatter(
        jnp.dot(gathered, dense.T, preferred_element_type=jnp.float32),
        "col",
        scatter_dimension=0,
        tiled=True,
    )
    return summed * factor


def solution(mesh):
    placed = (P("row", "col", None, None), P("row", "col"), P("row", "col"), P("col", "row", None))
    return jax.shard_map(
        local, mesh=mesh, in_specs=placed, out_specs=P("col", "row"), check_vma=False
    )
```

profile of v0, /device:TPU:3, one launch (start us, length us, event | category | flops | bytes accessed | tf_op | source)
XLA Modules:
  0.0 187.0 jit_solution(4186988405715089080)
XLA Ops:
  6.5 0.0 copy-start
  6.5 0.0 all-gather.2.cloned.1.call-start
  6.5 0.8 compare_select_fusion.1
  7.3 0.1 reshape.7
  7.4 25.6 %all_gather.6 = bf16[12,128,128]{2,1,0:T(8,128)(2,1)S(1)} all-gather(bf16[12,16,128]{2,1,0:T(8,128)(2,1)} %param.7), channel_id=1, replica_groups=mesh['row'=8,'col'=4] {'row'}, dimensions={1}, use_global_device_ids=true | all-gather | bytes 442368 | tf_op jit(solution)/shard_map/all_gather | solution.py:23
  33.0 0.6 gather_fusion
  33.6 0.0 copy-done
  33.7 0.4 fusion.5
  34.1 0.3 copy.6
  34.4 0.6 convolution_convert_fusion
  35.0 0.2 copy.11
  35.2 1.2 copy.8
  36.3 0.0 all-gather.2.cloned.1.call-update
  36.3 0.0 reduce-scatter.2.cloned.1.call-start
  36.4 106.6 %all-gather.2.cloned.1.call-done = bf16[2048,1536]{0,1:T(8,128)(2,1)} async-done(((bf16[256,1536]{0,1:T(8,128)(2,1)}), bf16[2048,1536]{0,1:T(8,128)(2,1)}) %all-gather.2.cloned.1.call-update) | async-done | bytes 6291472 | tf_op jit(solution)/shard_map/all_gather | solution.py:32
  143.0 6.0 %fusion.6 = f32[2048,256]{1,0:T(8,128)} fusion(bf16[2048,1536]{0,1:T(8,128)(2,1)} %all-gather.2.cloned.1.call-done, bf16[256,1536]{1,0:T(8,128)(2,1)S(1)} %bitcast.22), kind=kOutput, calls=%fused_computation.13 | convolution fusion | flops 1610612736 | bytes 9175040 | tf_op jit(solution)/shard_map/dot_general | solution.py:34
  149.0 0.0 reduce-scatter.2.cloned.1.call-update
  149.1 29.2 %reduce-scatter.2.cloned.1.call-done = f32[512,256]{1,0:T(8,128)} async-done(((f32[2048,256]{1,0:T(8,128)}), f32[512,256]{1,0:T(8,128)}) %reduce-scatter.2.cloned.1.call-update) | async-done | bytes 524304 | tf_op jit(solution)/shard_map/reduce_scatter | solution.py:33
  178.2 1.9 %broadcast_multiply_fusion = f32[512,256]{1,0:T(8,128)} fusion(f32[512,256]{1,0:T(8,128)} %reduce-scatter.2.cloned.1.call-done), kind=kLoop, calls=%fused_computation.5 | loop fusion | flops 131072 | bytes 1048576 | tf_op jit(solution)/shard_map/mul | solution.py:39
  (1 shorter events, 0.0 us)
Async XLA Ops:
  6.5 27.1 %copy-start = (bf16[2,6,128,128]{3,2,1,0:T(8,128)(2,1)S(1)}, bf16[2,6,128,128]{3,2,1,0:T(8,128)(2,1)}, u32[]{:S(2)}) copy-start(bf16[2,6,128,128]{3,2,1,0:T(8,128)(2,1)} %param.4) | copy-start | bytes 1179652
  6.5 136.5 %all-gather.2.cloned.1.call-start = ((), (), s32[]{:S(2)}) async-start(), calls=%async_computation.1 | async-start | bytes 7077888 | tf_op jit(solution)/shard_map/all_gather | solution.py:32
  36.3 141.9 %reduce-scatter.2.cloned.1.call-start = ((), (), s32[]{:S(2)}) async-start(), calls=%async_computation.2 | async-start | bytes 2621440 | tf_op jit(solution)/shard_map/reduce_scatter | solution.py:33
Sparse Core Ops, SparseCore 0:
  36.5 106.4 all-gather.1
  149.2 29.0 reduce-scatter.1
where the time goes:
time: 190 us; the launch traced here: 187 us
  waiting for transfers between devices  136 us (72%)
  blocking collectives  25.6 us (13%)
  between operations  13.4 us (7%)
  matrix products  7.02 us (4%)
  other arithmetic  2.69 us (1%)
  local copies, waits for them, and re-layouts  2.38 us (1%)
    all_gather x1, waiting for transfers between devices, local(): gathered = lax.all_gather(dense, 'row', axis=0, tiled=True)  107 us
    reduce_scatter x1, waiting for transfers between devices, local(): lax.psum_scatter(jnp.dot(gathered, dense.T, preferred_element_type=jnp.fl...  29.2 us
    all_gather x1, blocking collectives, local(): full_metric = lax.all_gather(metric, 'row', axis=1, tiled=True)  25.6 us
    dot_general x1, matrix products, local(): jnp.dot(gathered, dense.T, preferred_element_type=jnp.float32)  6.04 us
  transfers between devices with their start and end apart: 2, of which 2 were waited for; matrix products, arithmetic and copies ran while one was open for 0% of the time, Pallas kernels for 0%

commit v1 on v0

v1 whole, which is shorter than its diff:
```python
import functools

import jax
import jax.numpy as jnp
from jax import lax
from jax.experimental import pallas as pl
from jax.experimental.pallas import tpu as pltpu
from jax.sharding import PartitionSpec as P

MESH = pl.DeviceIdType.MESH


def kernel(
    n, m, share, fit, metric, lst, cnt, out,
    mbuf, mfull, gat, note, notes, table, turned, wide, part, red,
    met_send, met_recv, fit_send, fit_recv, note_send, note_recv, table_sem, red_send, red_recv,
):
    atoms, slots, rows, aux = fit.shape
    blocks = metric.shape[0]
    half = n // 2
    hops = (half, n - 1 - half)
    row = lax.axis_index("row")
    col = lax.axis_index("col")

    def at_position(p):
        p = lax.rem(p + n, n)
        return jnp.where(p < (n + 1) // 2, 2 * p, 2 * (n - 1 - p) + 1)

    place = jnp.where(lax.rem(row, 2) == 0, row // 2, n - 1 - row // 2)

    def source(way, step):
        return at_position(place - step if way == 0 else place + step)

    def target(way):
        return at_position(place + 1 if way == 0 else place + n - 1)

    barrier = pltpu.get_barrier_semaphore()
    for k in range(1, n):
        pl.semaphore_signal(barrier, inc=1, device_id=(lax.rem(row + k, n), col), device_id_type=MESH)
    for k in range(1, m):
        pl.semaphore_signal(barrier, inc=1, device_id=(row, lax.rem(col + k, m)), device_id_type=MESH)
    note[...] = jnp.zeros_like(note)
    note[0:atoms, 0:slots] = lst[...]
    note[0:atoms, slots : slots + 1] = cnt[...]
    notes[row] = note[...]
    mbuf[row] = metric[...]
    pl.semaphore_wait(barrier, n + m - 2)

    def met_copy(way, step, src, owner):
        return pltpu.make_async_remote_copy(
            src_ref=src, dst_ref=mbuf.at[owner], send_sem=met_send.at[way, step],
            recv_sem=met_recv.at[way, step], device_id=(target(way), col), device_id_type=MESH,
        )

    def fit_copy(way, atom, step, src, owner):
        return pltpu.make_async_remote_copy(
            src_ref=src, dst_ref=gat.at[owner, atom], send_sem=fit_send.at[way, atom, step],
            recv_sem=fit_recv.at[way, atom, step], device_id=(target(way), col), device_id_type=MESH,
        )

    def note_copy(k):
        return pltpu.make_async_remote_copy(
            src_ref=note, dst_ref=notes.at[row], send_sem=note_send.at[k],
            recv_sem=note_recv.at[k], device_id=(lax.rem(row + k, n), col), device_id_type=MESH,
        )

    def reach(way, atom):
        return hops[(way + atom) % 2]

    for way in range(2):
        if hops[way] > 0:
            met_copy(way, 0, metric, row).start()
    for k in range(1, n):
        note_copy(k).start()
    for atom in range(atoms):
        for way in range(2):
            if reach(way, atom) > 0:
                fit_copy(way, atom, 0, fit.at[atom], row).start()

    for step in range(1, half + 1):
        for way in range(2):
            if step <= hops[way]:
                owner = source(way, step)
                met_copy(way, step - 1, mbuf.at[owner], owner).wait_recv()
                if step < hops[way]:
                    met_copy(way, step, mbuf.at[owner], owner).start()
    for k in range(1, n):
        note_copy(k).wait_recv()
    to_table = pltpu.make_async_copy(notes, table, table_sem)
    to_table.start()
    for q in range(blocks):
        mfull[q] = mbuf[:, q].reshape(aux, aux).astype(jnp.bfloat16)
    to_table.wait()

    def fitted(tile, owner, atom, s):
        return jnp.dot(
            tile, mfull[table[owner, atom, s]], preferred_element_type=jnp.float32
        ).astype(jnp.bfloat16)

    def send_part(a):
        dest = a // share
        return pltpu.make_async_remote_copy(
            src_ref=part.at[a], dst_ref=red.at[col, lax.rem(a, share)], send_sem=red_send.at[a],
            recv_sem=red_recv.at[col, lax.rem(a, share)], device_id=(row, dest), device_id_type=MESH,
        )

    def combine(left, owner, atom):
        count = table[owner, atom, slots]
        right = [
            wide[jnp.where(s < count, table[owner, atom, s], blocks)] for s in range(slots)
        ]
        a = owner * atoms + atom
        part[a] = jnp.dot(
            jnp.concatenate(left, axis=1), jnp.concatenate(right, axis=0),
            preferred_element_type=jnp.float32,
        )

        @pl.when(a // share != col)
        def _():
            send_part(a).start()

    def process(view, owner, atom):
        combine([fitted(view[s], owner, atom, s) for s in range(slots)], owner, atom)

    own = []
    for atom in range(atoms):
        own.append([fitted(fit[atom, s], row, atom, s) for s in range(slots)])
        for s in range(slots):
            turned[atom, s] = own[atom][s].T
        turned[atom, slots] = jnp.zeros((aux, rows), jnp.bfloat16)
    for q in range(blocks):
        for atom in range(atoms):
            where = jnp.int32(slots)
            for s in range(slots):
                hit = (table[row, atom, s] == q) & (s < table[row, atom, slots])
                where = jnp.where(hit, s, where)
            wide[q, :, atom * rows : (atom + 1) * rows] = turned[atom, where]
    wide[blocks] = jnp.zeros_like(wide[blocks])
    for atom in range(atoms):
        combine(own[atom], row, atom)

    def arrive(step, pairs):
        for way, atom, last in pairs:
            owner = source(way, step)
            fit_copy(way, atom, step - 1, gat.at[owner, atom], owner).wait_recv()
            if not last:
                fit_copy(way, atom, step, gat.at[owner, atom], owner).start()
        for way, atom, _ in pairs:
            owner = source(way, step)
            process(gat.at[owner, atom], owner, atom)

    every = [(way, atom) for atom in range(atoms) for way in range(2)]
    for step in range(1, half + 1):
        arrive(step, [(w, b, step == reach(w, b)) for w, b in every if step <= reach(w, b)])

    for j in range(share):
        total = part[col * share + j]
        for k in range(1, m):
            peer = lax.rem(col + k, m)
            pltpu.make_async_remote_copy(
                src_ref=part.at[0], dst_ref=red.at[peer, j], send_sem=red_send.at[0],
                recv_sem=red_recv.at[peer, j], device_id=(row, peer), device_id_type=MESH,
            ).wait_recv()
            total += red[peer, j]
        out[j * rows : (j + 1) * rows, :] = total

    for way in range(2):
        for step in range(hops[way]):
            met_copy(way, step, metric, row).wait_send()
        for atom in range(atoms):
            for step in range(reach(way, atom)):
                fit_copy(way, atom, step, fit.at[atom], row).wait_send()
    for k in range(1, n):
        note_copy(k).wait_send()

    @pl.loop(0, n * atoms)
    def _(a):
        @pl.when(a // share != col)
        def _():
            send_part(a).wait_send()


def local(n, m, fit, aux_list, aux_count, metric):
    atoms, slots, rows, aux = fit.shape
    blocks, depth, _ = metric.shape
    share = n * atoms // m
    if depth % 16:
        metric = metric.astype(jnp.float32)
    dma = pltpu.SemaphoreType.DMA
    vmem = pl.BlockSpec(memory_space=pltpu.VMEM)
    summed = pl.pallas_call(
        functools.partial(kernel, n, m, share),
        out_shape=jax.ShapeDtypeStruct((share * rows, atoms * rows), jnp.float32),
        in_specs=[vmem] * 4,
        out_specs=vmem,
        scratch_shapes=[
            pltpu.VMEM((n, blocks, depth, aux), metric.dtype),
            pltpu.VMEM((blocks, aux, aux), jnp.bfloat16),
            pltpu.VMEM((n, atoms, slots, rows, aux), jnp.bfloat16),
            pltpu.VMEM((8, 128), jnp.int32),
            pltpu.VMEM((n, 8, 128), jnp.int32),
            pltpu.SMEM((n, 8, 128), jnp.int32),
            pltpu.VMEM((atoms, slots + 1, aux, rows), jnp.bfloat16),
            pltpu.VMEM((blocks + 1, aux, atoms * rows), jnp.bfloat16),
            pltpu.VMEM((n * atoms, rows, atoms * rows), jnp.float32),
            pltpu.VMEM((m, share, rows, atoms * rows), jnp.float32),
            dma((2, n)),
            dma((2, n)),
            dma((2, atoms, n)),
            dma((2, atoms, n)),
            dma((n,)),
            dma((n,)),
            dma,
            dma((n * atoms,)),
            dma((m, share)),
        ],
        compiler_params=pltpu.CompilerParams(
            collective_id=0, has_side_effects=True, vmem_limit_bytes=48 * 1024 * 1024
        ),
        cost_estimate=pl.CostEstimate(
            flops=2 * n * atoms * slots * rows * aux * (aux + atoms * rows),
            bytes_accessed=2 * n * atoms * slots * rows * aux,
            transcendentals=0,
        ),
    )(fit, metric, aux_list, aux_count)
    return summed * (1.0 / (slots * m * aux) ** 0.5)


def solution(mesh):
    placed = (P("row", "col", None, None), P("row", "col"), P("row", "col"), P("col", "row", None))
    return jax.shard_map(
        functools.partial(local, mesh.shape["row"], mesh.shape["col"]),
        mesh=mesh, in_specs=placed, out_specs=P("col", "row"), check_vma=False,
    )
```

time: 190 us -> 64.1 us (0.34); the launches traced: 187 us -> 63.7 us
  waiting for transfers between devices: 136 us -> 0 us
  Pallas kernels: 0 us -> 60.3 us
  blocking collectives: 25.6 us -> 0 us
  between operations: 13.4 us -> 0.01 us
  matrix products: 7.02 us -> 0 us
    all_gather x1 -> x0, waiting for transfers between devices: 107 us -> none  [local(): gathered = lax.all_gather(dense, 'row', axis=0, tiled=True)]
    pallas_call x0 -> x1, Pallas kernels: none -> 60.3 us  [local(): pl.pallas_call(functools.partial(kernel, n, m, share), out_shape=jax.Shap...]
    reduce_scatter x1 -> x0, waiting for transfers between devices: 29.2 us -> none  [local(): lax.psum_scatter(jnp.dot(gathered, dense.T, preferred_element_type=jnp.fl...]
    all_gather x1 -> x0, blocking collectives: 25.6 us -> none  [local(): full_metric = lax.all_gather(metric, 'row', axis=1, tiled=True)]
    dot_general x3 -> x0, matrix products: 7.02 us -> none  [the longest x1 6.04 us: local(): jnp.dot(gathered, dense.T, preferred_element_type=jnp.float32)]
    unnamed x3 -> x7, local copies, waits for them, and re-layouts: 0.21 us -> 2.55 us
  transfers between devices with their start and end apart: 2 -> 0, of which waited for: 2 -> 0; matrix products, arithmetic and copies ran while one was open for 0% -> 0% of each run, Pallas kernels for 0% -> 0%
where the time goes in v1:
time: 64.1 us; the launch traced here: 63.7 us
  Pallas kernels  60.3 us (94%)
  local copies, waits for them, and re-layouts  2.55 us (4%)
  other arithmetic  0.85 us (1%)
    pallas_call x1, Pallas kernels, local(): pl.pallas_call(functools.partial(kernel, n, m, share), out_shape=jax.Shap...  60.3 us
    unnamed x7, local copies, waits for them, and re-layouts  2.55 us

profile of v1, /device:TPU:3, one launch (start us, length us, event | category | flops | bytes accessed | tf_op | source)
XLA Modules:
  0.0 63.7 jit_solution(6959563662977068718)
XLA Ops:
  0.0 0.0 copy-start.2
  0.0 0.8 %copy.5.cnt = s32[2,1]{1,0:T(2,128)S(1)} copy(s32[2,1]{0,1:T(1,128)} %param.6) | data formatting | bytes 16 | tf_op args[2]
  0.8 0.0 copy-done.2
  0.8 0.0 copy-start
  0.8 1.0 %copy-done = bf16[2,6,128,128]{3,2,1,0:T(8,128)(2,1)S(1)} copy-done((bf16[2,6,128,128]{3,2,1,0:T(8,128)(2,1)S(1)}, bf16[2,6,128,128]{3,2,1,0:T(8,128)(2,1)}, u32[]{:S(2)}) %copy-start) | copy-done | bytes 393240
  1.8 0.0 copy-start.1
  1.8 0.8 %copy-done.1 = bf16[12,16,128]{2,1,0:T(8,128)(2,1)S(1)} copy-done((bf16[12,16,128]{2,1,0:T(8,128)(2,1)S(1)}, bf16[12,16,128]{2,1,0:T(8,128)(2,1)}, u32[]{:S(2)}) %copy-start.1) | copy-done | bytes 49176
  2.6 60.3 %shard_map.46 = f32[512,256]{1,0:T(8,128)S(1)} custom-call(bf16[2,6,128,128]{3,2,1,0:T(8,128)(2,1)S(1)} %copy-done, bf16[12,16,128]{2,1,0:T(8,128)(2,1)S(1)} %copy-done.1, s32[2,6]{1,0:T(2,128)S(1)} %copy-done.2, s32[2,1]{1,0:T(2,128)S(1)} %copy.5.cnt), custom_call_target="tpu_custom_call" | custom-call | flops 1207959552 | bytes 3145728 | tf_op jit(solution)/shard_map/pallas_call | solution.py:191
  62.8 0.8 %broadcast_multiply_fusion = f32[512,256]{1,0:T(8,128)} fusion(f32[512,256]{1,0:T(8,128)S(1)} %shard_map.46), kind=kLoop, calls=%fused_computation | loop fusion | flops 131072 | bytes 1048576 | tf_op jit(solution)/shard_map/mul | solution.py:226
Async XLA Ops:
  0.0 0.8 %copy-start.2 = (s32[2,6]{1,0:T(2,128)S(1)}, s32[2,6]{1,0:T(2,128)}, u32[]{:S(2)}) copy-start(s32[2,6]{1,0:T(2,128)} %lst.1) | copy-start | bytes 148
  0.8 1.0 %copy-start = (bf16[2,6,128,128]{3,2,1,0:T(8,128)(2,1)S(1)}, bf16[2,6,128,128]{3,2,1,0:T(8,128)(2,1)}, u32[]{:S(2)}) copy-start(bf16[2,6,128,128]{3,2,1,0:T(8,128)(2,1)} %fit.1) | copy-start | bytes 1179652
  1.8 0.8 %copy-start.1 = (bf16[12,16,128]{2,1,0:T(8,128)(2,1)S(1)}, bf16[12,16,128]{2,1,0:T(8,128)(2,1)}, u32[]{:S(2)}) copy-start(bf16[12,16,128]{2,1,0:T(8,128)(2,1)} %metric.1) | copy-start | bytes 147460

commit v2 on v1

--- a/solution.py
+++ b/solution.py
@@ -13,10 +13,13 @@
 def kernel(
     n, m, share, fit, metric, lst, cnt, out,
     mbuf, mfull, gat, note, notes, table, turned, wide, part, red,
-    met_send, met_recv, fit_send, fit_recv, note_send, note_recv, table_sem, red_send, red_recv,
+    keep_sem, met_send, met_recv, fit_send, fit_recv, note_send, note_recv, table_sem, red_send, red_recv,
 ):
     atoms, slots, rows, aux = fit.shape
     blocks = metric.shape[0]
+    cuts = 3 if slots % 3 == 0 else 1
+    span = slots // cuts
+    pieces = atoms * cuts
     half = n // 2
     hops = (half, n - 1 - half)
     row = lax.axis_index("row")
@@ -41,9 +44,12 @@
         pl.semaphore_signal(barrier, inc=1, device_id=(row, lax.rem(col + k, m)), device_id_type=MESH)
     note[...] = jnp.zeros_like(note)
     note[0:atoms, 0:slots] = lst[...]
-    note[0:atoms, slots : slots + 1] = cnt[...]
+    note[atoms : atoms + 1, 0:atoms] = cnt[...]
     notes[row] = note[...]
-    mbuf[row] = metric[...]
+    keep_fit = pltpu.make_async_copy(fit, gat.at[row], keep_sem.at[0])
+    keep_fit.start()
+    keep_metric = pltpu.make_async_copy(metric, mbuf.at[row], keep_sem.at[1])
+    keep_metric.start()
     pl.semaphore_wait(barrier, n + m - 2)
 
     def met_copy(way, step, src, owner):
@@ -52,10 +58,14 @@
             recv_sem=met_recv.at[way, step], device_id=(target(way), col), device_id_type=MESH,
         )
 
-    def fit_copy(way, atom, step, src, owner):
-        return pltpu.make_async_remote_copy(
-            src_ref=src, dst_ref=gat.at[owner, atom], send_sem=fit_send.at[way, atom, step],
-            recv_sem=fit_recv.at[way, atom, step], device_id=(target(way), col), device_id_type=MESH,
+    def piece(ref, u):
+        return ref.at[u // cuts, pl.ds((u % cuts) * span, span)]
+
+    def fit_copy(way, u, step, owner):
+        src = fit if step == 0 else gat.at[owner]
+        return pltpu.make_async_remote_copy(
+            src_ref=piece(src, u), dst_ref=piece(gat.at[owner], u), send_sem=fit_send.at[way, u, step],
+            recv_sem=fit_recv.at[way, u, step], device_id=(target(way), col), device_id_type=MESH,
         )
 
     def note_copy(k):
@@ -64,19 +74,26 @@
             recv_sem=note_recv.at[k], device_id=(lax.rem(row + k, n), col), device_id_type=MESH,
         )
 
-    def reach(way, atom):
-        return hops[(way + atom) % 2]
+    def reach(way, u):
+        return hops[(way + u) % 2]
+
+    def send_own(u):
+        for way in range(2):
+            if reach(way, u) > 0:
+                fit_copy(way, u, 0, row).start()
+
+    def arrive(way, u, step):
+        owner = source(way, step)
+        fit_copy(way, u, step - 1, owner).wait_recv()
+        if step < reach(way, u):
+            fit_copy(way, u, step, owner).start()
 
     for way in range(2):
         if hops[way] > 0:
             met_copy(way, 0, metric, row).start()
+    send_own(0)
     for k in range(1, n):
         note_copy(k).start()
-    for atom in range(atoms):
-        for way in range(2):
-            if reach(way, atom) > 0:
-                fit_copy(way, atom, 0, fit.at[atom], row).start()
-
     for step in range(1, half + 1):
         for way in range(2):
             if step <= hops[way]:
@@ -84,10 +101,20 @@
                 met_copy(way, step - 1, mbuf.at[owner], owner).wait_recv()
                 if step < hops[way]:
                     met_copy(way, step, mbuf.at[owner], owner).start()
+        if step < pieces:
+            send_own(step)
+    for u in range(half + 1, pieces):
+        send_own(u)
     for k in range(1, n):
         note_copy(k).wait_recv()
     to_table = pltpu.make_async_copy(notes, table, table_sem)
     to_table.start()
+    keep_fit.wait()
+    keep_metric.wait()
+    for u in range(pieces):
+        for way in range(2):
+            if reach(way, u) > 0:
+                arrive(way, u, 1)
     for q in range(blocks):
         mfull[q] = mbuf[:, q].reshape(aux, aux).astype(jnp.bfloat16)
     to_table.wait()
@@ -105,7 +132,7 @@
         )
 
     def combine(left, owner, atom):
-        count = table[owner, atom, slots]
+        count = table[owner, atoms, atom]
         right = [
             wide[jnp.where(s < count, table[owner, atom, s], blocks)] for s in range(slots)
         ]
@@ -119,12 +146,12 @@
         def _():
             send_part(a).start()
 
-    def process(view, owner, atom):
-        combine([fitted(view[s], owner, atom, s) for s in range(slots)], owner, atom)
+    def process(owner, atom):
+        combine([fitted(gat[owner, atom, s], owner, atom, s) for s in range(slots)], owner, atom)
 
     own = []
     for atom in range(atoms):
-        own.append([fitted(fit[atom, s], row, atom, s) for s in range(slots)])
+        own.append([fitted(gat[row, atom, s], row, atom, s) for s in range(slots)])
         for s in range(slots):
             turned[atom, s] = own[atom][s].T
         turned[atom, slots] = jnp.zeros((aux, rows), jnp.bfloat16)
@@ -132,26 +159,23 @@
         for atom in range(atoms):
             where = jnp.int32(slots)
             for s in range(slots):
-                hit = (table[row, atom, s] == q) & (s < table[row, atom, slots])
+                hit = (table[row, atom, s] == q) & (s < table[row, atoms, atom])
                 where = jnp.where(hit, s, where)
             wide[q, :, atom * rows : (atom + 1) * rows] = turned[atom, where]
     wide[blocks] = jnp.zeros_like(wide[blocks])
     for atom in range(atoms):
         combine(own[atom], row, atom)
 
-    def arrive(step, pairs):
-        for way, atom, last in pairs:
-            owner = source(way, step)
-            fit_copy(way, atom, step - 1, gat.at[owner, atom], owner).wait_recv()
-            if not last:
-                fit_copy(way, atom, step, gat.at[owner, atom], owner).start()
-        for way, atom, _ in pairs:
-            owner = source(way, step)
-            process(gat.at[owner, atom], owner, atom)
-
-    every = [(way, atom) for atom in range(atoms) for way in range(2)]
     for step in range(1, half + 1):
-        arrive(step, [(w, b, step == reach(w, b)) for w, b in every if step <= reach(w, b)])
+        both = step <= min(hops)
+        for atom in range(atoms):
+            for u in range(atom * cuts, (atom + 1) * cuts):
+                for way in range(2):
+                    if 1 < step <= reach(way, u):
+                        arrive(way, u, step)
+            process(source(0, step), atom)
+            if both:
+                process(source(1, step), atom)
 
     for j in range(share):
         total = part[col * share + j]
@@ -167,9 +191,9 @@
     for way in range(2):
         for step in range(hops[way]):
             met_copy(way, step, metric, row).wait_send()
-        for atom in range(atoms):
-            for step in range(reach(way, atom)):
-                fit_copy(way, atom, step, fit.at[atom], row).wait_send()
+        for u in range(pieces):
+            for step in range(reach(way, u)):
+                fit_copy(way, u, step, row).wait_send()
     for k in range(1, n):
         note_copy(k).wait_send()
 
@@ -191,7 +215,7 @@
     summed = pl.pallas_call(
         functools.partial(kernel, n, m, share),
         out_shape=jax.ShapeDtypeStruct((share * rows, atoms * rows), jnp.float32),
-        in_specs=[vmem] * 4,
+        in_specs=[pl.BlockSpec(memory_space=pltpu.HBM)] * 2 + [vmem] * 2,
         out_specs=vmem,
         scratch_shapes=[
             pltpu.VMEM((n, blocks, depth, aux), metric.dtype),
@@ -204,10 +228,11 @@
             pltpu.VMEM((blocks + 1, aux, atoms * rows), jnp.bfloat16),
             pltpu.VMEM((n * atoms, rows, atoms * rows), jnp.float32),
             pltpu.VMEM((m, share, rows, atoms * rows), jnp.float32),
+            dma((2,)),
             dma((2, n)),
             dma((2, n)),
-            dma((2, atoms, n)),
-            dma((2, atoms, n)),
+            dma((2, atoms * slots, n)),
+            dma((2, atoms * slots, n)),
             dma((n,)),
             dma((n,)),
             dma,
@@ -222,7 +247,7 @@
             bytes_accessed=2 * n * atoms * slots * rows * aux,
             transcendentals=0,
         ),
-    )(fit, metric, aux_list, aux_count)
+    )(fit, metric, aux_list, aux_count.T)
     return summed * (1.0 / (slots * m * aux) ** 0.5)
 
 

time: 64.1 us -> 58.8 us (0.917)
  Pallas kernels: 60.3 us -> 54.9 us
    pallas_call x1, Pallas kernels: 60.3 us -> 54.9 us  [local(): pl.pallas_call(functools.partial(kernel, n, m, share), out_shape=jax.Shap...]
    unnamed x7 -> x8, local copies, waits for them, and re-layouts: 2.55 us -> 2.49 us
where the time goes in v2:
time: 58.8 us; the launch traced here: 58.2 us
  Pallas kernels  54.9 us (93%)
  local copies, waits for them, and re-layouts  2.49 us (4%)
  other arithmetic  0.85 us (1%)
    pallas_call x1, Pallas kernels, local(): pl.pallas_call(functools.partial(kernel, n, m, share), out_shape=jax.Shap...  54.9 us
    unnamed x8, local copies, waits for them, and re-layouts  2.49 us

profile of v2, /device:TPU:3, one launch (start us, length us, event | category | flops | bytes accessed | tf_op | source)
XLA Modules:
  0.0 58.2 jit_solution(16852034245179144359)
XLA Ops:
  0.0 0.0 copy-start.3
  0.0 0.0 copy-start.2
  0.0 0.7 %copy-done.3 = s32[2,1]{0,1:T(1,128)S(1)} copy-done((s32[2,1]{0,1:T(1,128)S(1)}, s32[2,1]{0,1:T(1,128)}, u32[]{:S(2)}) %copy-start.3) | copy-done | bytes 32
  0.7 0.0 copy-done.2
  0.7 0.0 copy-start
  0.7 1.0 %copy-done = bf16[2,6,128,128]{3,2,1,0:T(8,128)(2,1)S(1)} copy-done((bf16[2,6,128,128]{3,2,1,0:T(8,128)(2,1)S(1)}, bf16[2,6,128,128]{3,2,1,0:T(8,128)(2,1)}, u32[]{:S(2)}) %copy-start) | copy-done | bytes 393240
  1.7 0.0 copy-start.1
  1.7 0.8 %copy-done.1 = bf16[12,16,128]{2,1,0:T(8,128)(2,1)S(1)} copy-done((bf16[12,16,128]{2,1,0:T(8,128)(2,1)S(1)}, bf16[12,16,128]{2,1,0:T(8,128)(2,1)}, u32[]{:S(2)}) %copy-start.1) | copy-done | bytes 49176
  2.5 54.9 %shard_map.46 = f32[512,256]{1,0:T(8,128)S(1)} custom-call(bf16[2,6,128,128]{3,2,1,0:T(8,128)(2,1)S(1)} %copy-done, bf16[12,16,128]{2,1,0:T(8,128)(2,1)S(1)} %copy-done.1, s32[2,6]{1,0:T(2,128)S(1)} %copy-done.2, s32[1,2]{1,0:T(1,128)S(1)} %bitcast.1), custom_call_target="tpu_custom_call" | custom-call | flops 1207959552 | bytes 3145728 | tf_op jit(solution)/shard_map/pallas_call | solution.py:215
  57.4 0.8 %broadcast_multiply_fusion = f32[512,256]{1,0:T(8,128)} fusion(f32[512,256]{1,0:T(8,128)S(1)} %shard_map.46), kind=kLoop, calls=%fused_computation | loop fusion | flops 131072 | bytes 1048576 | tf_op jit(solution)/shard_map/mul | solution.py:251
Async XLA Ops:
  0.0 0.7 %copy-start.3 = (s32[2,1]{0,1:T(1,128)S(1)}, s32[2,1]{0,1:T(1,128)}, u32[]{:S(2)}) copy-start(s32[2,1]{0,1:T(1,128)} %param.6) | copy-start | bytes 28
  0.0 0.7 %copy-start.2 = (s32[2,6]{1,0:T(2,128)S(1)}, s32[2,6]{1,0:T(2,128)}, u32[]{:S(2)}) copy-start(s32[2,6]{1,0:T(2,128)} %lst.1) | copy-start | bytes 148
  0.7 1.0 %copy-start = (bf16[2,6,128,128]{3,2,1,0:T(8,128)(2,1)S(1)}, bf16[2,6,128,128]{3,2,1,0:T(8,128)(2,1)}, u32[]{:S(2)}) copy-start(bf16[2,6,128,128]{3,2,1,0:T(8,128)(2,1)} %fit.1) | copy-start | bytes 1179652
  1.7 0.8 %copy-start.1 = (bf16[12,16,128]{2,1,0:T(8,128)(2,1)S(1)}, bf16[12,16,128]{2,1,0:T(8,128)(2,1)}, u32[]{:S(2)}) copy-start(bf16[12,16,128]{2,1,0:T(8,128)(2,1)} %metric.1) | copy-start | bytes 147460

commit v3 on v2

--- a/solution.py
+++ b/solution.py
@@ -12,14 +12,15 @@
 
 def kernel(
     n, m, share, fit, metric, lst, cnt, out,
-    mbuf, mfull, gat, note, notes, table, turned, wide, part, red,
-    keep_sem, met_send, met_recv, fit_send, fit_recv, note_send, note_recv, table_sem, red_send, red_recv,
+    mbuf, mfull, gat, note, notes, table, turned, wide, part, mid, red,
+    keep_sem, met_send, met_recv, fit_send, fit_recv, note_send, note_recv, table_sem, mid_recv, red_send, red_recv,
 ):
     atoms, slots, rows, aux = fit.shape
     blocks = metric.shape[0]
-    cuts = 3 if slots % 3 == 0 else 1
-    span = slots // cuts
+    cuts = 4
+    span = rows // cuts
     pieces = atoms * cuts
+    feed = 2
     half = n // 2
     hops = (half, n - 1 - half)
     row = lax.axis_index("row")
@@ -59,7 +60,7 @@
         )
 
     def piece(ref, u):
-        return ref.at[u // cuts, pl.ds((u % cuts) * span, span)]
+        return ref.at[u // cuts, :, pl.ds((u % cuts) * span, span)]
 
     def fit_copy(way, u, step, owner):
         src = fit if step == 0 else gat.at[owner]
@@ -91,7 +92,8 @@
     for way in range(2):
         if hops[way] > 0:
             met_copy(way, 0, metric, row).start()
-    send_own(0)
+    for u in range(min(feed, pieces)):
+        send_own(u)
     for k in range(1, n):
         note_copy(k).start()
     for step in range(1, half + 1):
@@ -101,9 +103,9 @@
                 met_copy(way, step - 1, mbuf.at[owner], owner).wait_recv()
                 if step < hops[way]:
                     met_copy(way, step, mbuf.at[owner], owner).start()
-        if step < pieces:
-            send_own(step)
-    for u in range(half + 1, pieces):
+        for u in range(step * feed, min(pieces, (step + 1) * feed)):
+            send_own(u)
+    for u in range((half + 1) * feed, pieces):
         send_own(u)
     for k in range(1, n):
         note_copy(k).wait_recv()
@@ -124,30 +126,67 @@
             tile, mfull[table[owner, atom, s]], preferred_element_type=jnp.float32
         ).astype(jnp.bfloat16)
 
-    def send_part(a):
-        dest = a // share
-        return pltpu.make_async_remote_copy(
-            src_ref=part.at[a], dst_ref=red.at[col, lax.rem(a, share)], send_sem=red_send.at[a],
-            recv_sem=red_recv.at[col, lax.rem(a, share)], device_id=(row, dest), device_id_type=MESH,
-        )
-
-    def combine(left, owner, atom):
+    twin = col + 1 - 2 * lax.rem(col, 2)
+
+    def send_part(a, low, size):
+        lines = pl.ds(low, size)
+        return pltpu.make_async_remote_copy(
+            src_ref=part.at[a, lines], dst_ref=red.at[col, lax.rem(a, share), lines], send_sem=red_send.at[a],
+            recv_sem=red_recv.at[col, lax.rem(a, share)], device_id=(row, a // share), device_id_type=MESH,
+        )
+
+    def send_twin(a, low, size):
+        lines = pl.ds(low, size)
+        return pltpu.make_async_remote_copy(
+            src_ref=part.at[a, lines], dst_ref=mid.at[a, lines], send_sem=red_send.at[a],
+            recv_sem=mid_recv.at[a, low // span], device_id=(row, twin), device_id_type=MESH,
+        )
+
+    def far(a):
+        return (a // share) // 2 != col // 2
+
+    def same(a):
+        return lax.rem(a // share, 2) == lax.rem(col, 2)
+
+    waiting = []
+
+    def pass_on():
+        a, low, size = waiting.pop(0)
+
+        @pl.when(far(a) & same(a))
+        def _():
+            send_twin(a, low, size).wait_recv()
+            part[a, low : low + size] += mid[a, low : low + size]
+            send_part(a, low, size).start()
+
+    def combine(left, owner, atom, low=0, size=rows):
         count = table[owner, atoms, atom]
         right = [
             wide[jnp.where(s < count, table[owner, atom, s], blocks)] for s in range(slots)
         ]
         a = owner * atoms + atom
-        part[a] = jnp.dot(
+        part[a, low : low + size] = jnp.dot(
             jnp.concatenate(left, axis=1), jnp.concatenate(right, axis=0),
             preferred_element_type=jnp.float32,
         )
 
-        @pl.when(a // share != col)
+        @pl.when(far(a) & jnp.logical_not(same(a)))
         def _():
-            send_part(a).start()
-
-    def process(owner, atom):
-        combine([fitted(gat[owner, atom, s], owner, atom, s) for s in range(slots)], owner, atom)
+            send_twin(a, low, size).start()
+
+        @pl.when(a // share == twin)
+        def _():
+            send_part(a, low, size).start()
+
+        waiting.append((a, low, size))
+        if len(waiting) > 2:
+            pass_on()
+
+    def process(owner, atom, low=0, size=rows):
+        left = [
+            fitted(gat[owner, atom, s, low : low + size, :], owner, atom, s) for s in range(slots)
+        ]
+        combine(left, owner, atom, low, size)
 
     own = []
     for atom in range(atoms):
@@ -166,21 +205,25 @@
     for atom in range(atoms):
         combine(own[atom], row, atom)
 
-    for step in range(1, half + 1):
-        both = step <= min(hops)
+    for step in range(1, min(hops) + 1):
         for atom in range(atoms):
             for u in range(atom * cuts, (atom + 1) * cuts):
                 for way in range(2):
-                    if 1 < step <= reach(way, u):
+                    if step > 1:
                         arrive(way, u, step)
-            process(source(0, step), atom)
-            if both:
-                process(source(1, step), atom)
-
+            for way in range(2):
+                process(source(way, step), atom)
+    if hops[0] > hops[1]:
+        for u in range(pieces):
+            if half > 1:
+                arrive(u % 2, u, half)
+            process(source(0, half), u // cuts, (u % cuts) * span, span)
+
+    while waiting:
+        pass_on()
     for j in range(share):
         total = part[col * share + j]
-        for k in range(1, m):
-            peer = lax.rem(col + k, m)
+        for peer in [twin] + [lax.rem(col + k, m) for k in range(2, m, 2)]:
             pltpu.make_async_remote_copy(
                 src_ref=part.at[0], dst_ref=red.at[peer, j], send_sem=red_send.at[0],
                 recv_sem=red_recv.at[peer, j], device_id=(row, peer), device_id_type=MESH,
@@ -201,7 +244,7 @@
     def _(a):
         @pl.when(a // share != col)
         def _():
-            send_part(a).wait_send()
+            send_part(a, 0, rows).wait_send()
 
 
 def local(n, m, fit, aux_list, aux_count, metric):
@@ -227,15 +270,17 @@
             pltpu.VMEM((atoms, slots + 1, aux, rows), jnp.bfloat16),
             pltpu.VMEM((blocks + 1, aux, atoms * rows), jnp.bfloat16),
             pltpu.VMEM((n * atoms, rows, atoms * rows), jnp.float32),
+            pltpu.VMEM((n * atoms, rows, atoms * rows), jnp.float32),
             pltpu.VMEM((m, share, rows, atoms * rows), jnp.float32),
             dma((2,)),
             dma((2, n)),
             dma((2, n)),
-            dma((2, atoms * slots, n)),
-            dma((2, atoms * slots, n)),
+            dma((2, 4 * atoms, n)),
+            dma((2, 4 * atoms, n)),
             dma((n,)),
             dma((n,)),
             dma,
+            dma((n * atoms, 4)),
             dma((n * atoms,)),
             dma((m, share)),
         ],

time: 58.8 us -> 54.2 us (0.922)
  Pallas kernels: 54.9 us -> 50.6 us
    pallas_call x1, Pallas kernels: 54.9 us -> 50.6 us  [local(): pl.pallas_call(functools.partial(kernel, n, m, share), out_shape=jax.Shap...]
where the time goes in v3:
time: 54.2 us; the launch traced here: 53.9 us
  Pallas kernels  50.6 us (93%)
  local copies, waits for them, and re-layouts  2.49 us (5%)
  other arithmetic  0.85 us (2%)
    pallas_call x1, Pallas kernels, local(): pl.pallas_call(functools.partial(kernel, n, m, share), out_shape=jax.Shap...  50.6 us
    unnamed x8, local copies, waits for them, and re-layouts  2.49 us

profile of v3, /device:TPU:3, one launch (start us, length us, event | category | flops | bytes accessed | tf_op | source)
XLA Modules:
  0.0 53.9 jit_solution(5590488388716824425)
XLA Ops:
  0.0 0.0 copy-start.3
  0.0 0.0 copy-start.2
  0.0 0.7 %copy-done.3 = s32[2,1]{0,1:T(1,128)S(1)} copy-done((s32[2,1]{0,1:T(1,128)S(1)}, s32[2,1]{0,1:T(1,128)}, u32[]{:S(2)}) %copy-start.3) | copy-done | bytes 32
  0.7 0.0 copy-done.2
  0.7 0.0 copy-start
  0.7 1.0 %copy-done = bf16[2,6,128,128]{3,2,1,0:T(8,128)(2,1)S(1)} copy-done((bf16[2,6,128,128]{3,2,1,0:T(8,128)(2,1)S(1)}, bf16[2,6,128,128]{3,2,1,0:T(8,128)(2,1)}, u32[]{:S(2)}) %copy-start) | copy-done | bytes 393240
  1.7 0.0 copy-start.1
  1.7 0.8 %copy-done.1 = bf16[12,16,128]{2,1,0:T(8,128)(2,1)S(1)} copy-done((bf16[12,16,128]{2,1,0:T(8,128)(2,1)S(1)}, bf16[12,16,128]{2,1,0:T(8,128)(2,1)}, u32[]{:S(2)}) %copy-start.1) | copy-done | bytes 49176
  2.5 50.6 %shard_map.46 = f32[512,256]{1,0:T(8,128)S(1)} custom-call(bf16[2,6,128,128]{3,2,1,0:T(8,128)(2,1)S(1)} %copy-done, bf16[12,16,128]{2,1,0:T(8,128)(2,1)S(1)} %copy-done.1, s32[2,6]{1,0:T(2,128)S(1)} %copy-done.2, s32[1,2]{1,0:T(1,128)S(1)} %bitcast.1), custom_call_target="tpu_custom_call" | custom-call | flops 1207959552 | bytes 3145728 | tf_op jit(solution)/shard_map/pallas_call | solution.py:258
  53.1 0.8 %broadcast_multiply_fusion = f32[512,256]{1,0:T(8,128)} fusion(f32[512,256]{1,0:T(8,128)S(1)} %shard_map.46), kind=kLoop, calls=%fused_computation | loop fusion | flops 131072 | bytes 1048576 | tf_op jit(solution)/shard_map/mul | solution.py:296
Async XLA Ops:
  0.0 0.7 %copy-start.3 = (s32[2,1]{0,1:T(1,128)S(1)}, s32[2,1]{0,1:T(1,128)}, u32[]{:S(2)}) copy-start(s32[2,1]{0,1:T(1,128)} %param.6) | copy-start | bytes 28
  0.0 0.7 %copy-start.2 = (s32[2,6]{1,0:T(2,128)S(1)}, s32[2,6]{1,0:T(2,128)}, u32[]{:S(2)}) copy-start(s32[2,6]{1,0:T(2,128)} %lst.1) | copy-start | bytes 148
  0.7 1.0 %copy-start = (bf16[2,6,128,128]{3,2,1,0:T(8,128)(2,1)S(1)}, bf16[2,6,128,128]{3,2,1,0:T(8,128)(2,1)}, u32[]{:S(2)}) copy-start(bf16[2,6,128,128]{3,2,1,0:T(8,128)(2,1)} %fit.1) | copy-start | bytes 1179652
  1.7 0.8 %copy-start.1 = (bf16[12,16,128]{2,1,0:T(8,128)(2,1)S(1)}, bf16[12,16,128]{2,1,0:T(8,128)(2,1)}, u32[]{:S(2)}) copy-start(bf16[12,16,128]{2,1,0:T(8,128)(2,1)} %metric.1) | copy-start | bytes 147460
